TPU v7x, 256 devices: a whole 4x4x8 slice. The times are simulated.
256 devices in a mesh: seq: 64 (over y, z, core), ch: 4 (over x).
Axes of the slice: x: 4, y: 4, z: 8, core: 2. Of those that a mesh axis runs over, the one named last changes fastest.
Arguments:
- stream: bfloat16 [8192, 8192], P('seq', 'ch'), may hold values from -3000 to 3000
- norm_gain: float32 [8192], P('ch'), may hold values from 0.5 to 1.5
- gate_act: bfloat16 [8192, 8192], P('seq', 'ch'), may hold values from -6 to 6
- decay_rate: float32 [8192, 16], P('ch'), may hold values from 0 to 1, as said below
- residue: float32 [8192, 16], P('ch'), may hold values from -1.5 to 1.5
- skip_gain: float32 [8192], P('ch'), may hold values from 0.5 to 1.5
Outputs:
- gated_output: bfloat16 [8192, 8192], P('seq', 'ch')
Inputs may be any that keep to these rules, and one draw needn't show every extreme that they name: `decay_rate`: every rate is positive.
All inputs are finite; a program needn't handle non-finite values.
Results may differ from a plain program's by a relative error of at most 0.012.
Values may be sent and summed in bfloat16 or wider, within the bound.
A program may use at most 128 MiB of HBM per device.

v0:
```python
import functools
import math

import jax
import jax.numpy as jnp
import numpy as np
from jax import lax
from jax.experimental import pallas as pl
from jax.experimental.pallas import tpu as pltpu
from jax.sharding import PartitionSpec as P

MESH = pl.DeviceIdType.MESH
EPS = 1e-06
LANES = 128
WIRE = jnp.bfloat16
F32 = jnp.float32
BF16 = jnp.bfloat16


def half_tables(length):
    k = np.arange(length)[:, None] + 0.5
    t = np.arange(length)[None, :]
    angle = np.pi * k * t / length
    forward = np.concatenate([np.cos(angle), -np.sin(angle)], axis=0)
    inverse = np.concatenate([np.cos(angle.T), -np.sin(angle.T)], axis=1) / length

    def split(table):
        high = table.astype(BF16)
        low = (table - high.astype(np.float64)).astype(BF16)
        return np.concatenate([high, low], axis=1)

    return split(forward), split(inverse)


def one_minus_exp_neg(z):
    series = jnp.ones_like(z)
    for n in range(10, 1, -1):
        series = 1.0 - z * series * (1.0 / n)
    return jnp.where(z < 0.5, z * series, 1.0 - jnp.exp(-z))


def total_of(items):
    items = list(items)
    while len(items) > 1:
        items = [a + b for a, b in zip(items[::2], items[1::2])] + ([items[-1]] if len(items) % 2 else [])
    return items[0]


def kernel(nx, ny, nj, modes, width,
           x_hbm, rate_hbm, res_hbm, gain_hbm, skip_hbm, gate_hbm, fwd_hbm, inv_hbm, out_ref,
           x_v, gate_v, rate_v, res_v, gain_v, skip_v, fwd_v, inv_v,
           sqacc_v, sq_v, scol_v, pow_v, taps_v, xn_v, conv_v, srow_v,
           st_out, st_in, tot_v, pre_v, ca_out, ca_in,
           in_sem, x_sem, sq_send, sq_recv, st_send, st_recv, tot_send, tot_recv, ca_send, ca_recv):
    tokens, chans = x_v.shape
    blocks = chans // LANES
    mx = lax.axis_index("ch")
    seq = lax.axis_index("seq")
    my = seq // nj
    mj = lax.rem(seq, nj)

    def group_peer(k):
        return {"seq": my * nj + k}

    def spread(i):
        half = nj // 2
        return half + jnp.where(lax.rem(i, 2) == 1, (i + 1) // 2, -(i // 2))

    barrier = pltpu.get_barrier_semaphore()
    for d in range(1, nx):
        pl.semaphore_signal(barrier, inc=1, device_id={"ch": lax.rem(mx + d, nx)}, device_id_type=MESH)
    for d in range(1, ny):
        pl.semaphore_signal(barrier, inc=1, device_id={"seq": lax.rem(seq + d * nj, ny * nj)}, device_id_type=MESH)
    for d in range(1, nj):
        pl.semaphore_signal(barrier, inc=1, device_id=group_peer(lax.rem(mj + d, nj)), device_id_type=MESH)

    parts = x_sem.shape[0]
    rows_part = tokens // parts
    for p in range(parts):
        rows = pl.ds(p * rows_part, rows_part)
        pltpu.make_async_copy(x_hbm.at[rows], x_v.at[rows], x_sem.at[p]).start()
    staged = [(rate_hbm, rate_v), (res_hbm, res_v), (gain_hbm, gain_v), (skip_hbm, skip_v),
              (fwd_hbm, fwd_v), (inv_hbm, inv_v), (gate_hbm, gate_v)]
    staged = [pltpu.make_async_copy(a, b, in_sem.at[n]) for n, (a, b) in enumerate(staged)]
    for copy in staged:
        copy.start()

    tiles_part = rows_part // 16
    for p in range(parts):
        rows = pl.ds(p * rows_part, rows_part)
        pltpu.make_async_copy(x_hbm.at[rows], x_v.at[rows], x_sem.at[p]).wait()

        def square_rows(i, carry):
            part = pl.ds(pl.multiple_of(p * rows_part + i * 16, 16), 16)
            pieces = []
            for b in range(blocks):
                v = x_v[part, b * LANES:(b + 1) * LANES].astype(F32)
                pieces.append(v * v)
            sqacc_v[part, :] = total_of(pieces)
            return carry

        lax.fori_loop(0, tiles_part, square_rows, 0)
    turned = sqacc_v[...].T
    sq_v[mx] = total_of([turned[i * 8:(i + 1) * 8] for i in range(LANES // 8)])

    pl.semaphore_wait(barrier, nx + ny + nj - 3)
    sq_copies = []
    for d in range(1, nx):
        copy = pltpu.make_async_remote_copy(
            src_ref=sq_v.at[mx], dst_ref=sq_v.at[mx], send_sem=sq_send.at[d], recv_sem=sq_recv.at[mx],
            device_id={"ch": lax.rem(mx + d, nx)}, device_id_type=MESH)
        copy.start()
        sq_copies.append(copy)

    for copy in staged[:6]:
        copy.wait()
    step8 = lax.broadcasted_iota(jnp.int32, (8, LANES), 0).astype(F32)

    def rows_of(tile):
        return [jnp.broadcast_to(tile[m:m + 1, :], (8, LANES)) for m in range(modes)]

    def filter_block(b, carry):
        lanes = pl.ds(pl.multiple_of(b * LANES, LANES), LANES)
        rate = rate_v[:, lanes]
        weight = res_v[:, lanes] * jnp.sqrt(one_minus_exp_neg(2.0 * rate))
        jump = rows_of(jnp.exp(-8.0 * rate))
        terms = []
        for m in range(modes):
            power = jnp.exp(-rate[m:m + 1, :] * step8)
            pow_v[b * modes + m] = power
            terms.append(power * weight[m:m + 1, :])
        for t in range(tokens // 16):
            first = total_of(terms)
            terms = [a * c for a, c in zip(terms, jump)]
            second = total_of(terms)
            if t < tokens // 16 - 1:
                terms = [a * c for a, c in zip(terms, jump)]
            both = jnp.concatenate([first, second], axis=0)
            high = both.astype(BF16)
            taps_v[t * 16:(t + 1) * 16, lanes] = high
            taps_v[tokens + t * 16:tokens + (t + 1) * 16, lanes] = (both - high.astype(F32)).astype(BF16)
        return carry

    lax.fori_loop(0, blocks, filter_block, 0)

    for d in range(1, nx):
        src = lax.rem(mx + d, nx)
        pltpu.make_async_remote_copy(
            src_ref=sq_v.at[src], dst_ref=sq_v.at[src], send_sem=sq_send.at[d], recv_sem=sq_recv.at[src],
            device_id={"ch": src}, device_id_type=MESH).wait_recv()
    squares = jnp.sum(total_of([sq_v[i] for i in range(nx)]), axis=0, keepdims=True)
    scale = lax.rsqrt(squares / (nx * chans) + EPS)
    scol_v[...] = jnp.broadcast_to(scale, (tokens, LANES)).T

    def state_copy(b):
        return pltpu.make_async_remote_copy(
            src_ref=st_out.at[b], dst_ref=st_in.at[mj], send_sem=st_send.at[b], recv_sem=st_recv.at[mj],
            device_id=group_peer(b), device_id_type=MESH)

    def state_block(i, carry):
        b = lax.rem(mj + spread(i), nj)
        lanes = pl.ds(pl.multiple_of(b * LANES, LANES), LANES)
        rate = rate_v[:, lanes]
        jump = rows_of(jnp.exp(-8.0 * rate))
        gain = gain_v[pl.ds(b, 1), :]
        sums = [None] * modes
        for t in range(tokens // 16):
            value = x_v[t * 16:(t + 1) * 16, lanes].astype(F32) * scol_v[t * 16:(t + 1) * 16, :] * gain
            value = value.astype(BF16)
            xn_v[t * 16:(t + 1) * 16, lanes] = value
            value = value.astype(F32)
            for part in (value[:8], value[8:]):
                sums = [part if s is None else s * c + part for s, c in zip(sums, jump)]
        for m in range(modes):
            left = jnp.exp(-rate[m:m + 1, :] * (7.0 - step8))
            srow_v[m:m + 1, :] = jnp.sum(sums[m] * left, axis=0, keepdims=True)
        st_out[b] = srow_v[...].astype(st_out.dtype)

        @pl.when(i < nj - 1)
        def _():
            state_copy(b).start()

        return carry

    lax.fori_loop(0, nj, state_block, 0)
    st_in[mj] = st_out[mj]

    def local_conv(c, carry):
        lanes = pl.ds(pl.multiple_of(c * width, width), width)
        xn = xn_v[:, lanes]
        high = taps_v[:tokens, lanes]
        low = taps_v[tokens:, lanes]
        spec = jnp.dot(fwd_v[...], jnp.concatenate([xn, xn], axis=0), preferred_element_type=F32)
        filt = jnp.dot(fwd_v[...], jnp.concatenate([high, high], axis=0), preferred_element_type=F32)
        filt = filt + jnp.dot(fwd_v[:, :tokens], low, preferred_element_type=F32)
        xr, xi = spec[:tokens], spec[tokens:]
        fr, fi = filt[:tokens], filt[tokens:]
        prod = jnp.concatenate([xr * fr - xi * fi, xr * fi + xi * fr], axis=0)
        phigh = prod.astype(BF16)
        plow = (prod - phigh.astype(F32)).astype(BF16)
        conv = jnp.dot(inv_v[...], jnp.concatenate([phigh, phigh], axis=0), preferred_element_type=F32)
        conv = conv + jnp.dot(inv_v[:, :2 * tokens], plow, preferred_element_type=F32)
        per = width // LANES
        skip = jnp.concatenate([skip_v[pl.ds(c * per + n, 1), :] for n in range(per)], axis=1)
        conv_v[:, lanes] = conv + skip * xn.astype(F32)
        return carry

    chunks = chans // width
    cut1, cut2 = chunks // 2, (3 * chunks) // 4
    lax.fori_loop(0, cut1, local_conv, 0)

    own = pl.ds(pl.multiple_of(mj * LANES, LANES), LANES)
    rate = rate_v[:, own]
    decay = jnp.exp(-float(tokens) * rate)

    def scan_group(k, state):
        @pl.when(k != mj)
        def _():
            pltpu.make_async_remote_copy(
                src_ref=st_out.at[k], dst_ref=st_in.at[k], send_sem=st_send.at[k], recv_sem=st_recv.at[k],
                device_id=group_peer(k), device_id_type=MESH).wait_recv()

        pre_v[k] = state
        return state * decay + st_in[k].astype(F32)

    tot_v[my] = lax.fori_loop(0, nj, scan_group, jnp.zeros((modes, LANES), F32))

    tot_copies = []
    for d in range(1, ny):
        copy = pltpu.make_async_remote_copy(
            src_ref=tot_v.at[my], dst_ref=tot_v.at[my], send_sem=tot_send.at[d], recv_sem=tot_recv.at[my],
            device_id={"seq": lax.rem(seq + d * nj, ny * nj)}, device_id_type=MESH)
        copy.start()
        tot_copies.append(copy)

    lax.fori_loop(cut1, cut2, local_conv, 0)

    for d in range(1, ny):
        src = lax.rem(my + d, ny)
        pltpu.make_async_remote_copy(
            src_ref=tot_v.at[src], dst_ref=tot_v.at[src], send_sem=tot_send.at[d], recv_sem=tot_recv.at[src],
            device_id={"seq": src * nj + mj}, device_id_type=MESH).wait_recv()
    before = jnp.zeros((modes, LANES), F32)
    for k in range(ny):
        steps = jnp.maximum(my - 1 - k, 0) * (nj * tokens)
        live = (k < my).astype(F32)
        before = before + live * jnp.exp(-rate * steps.astype(F32)) * tot_v[k]
    scaled = res_v[:, own] * jnp.sqrt(one_minus_exp_neg(2.0 * rate)) * jnp.exp(-rate)

    def carry_copy(k):
        return pltpu.make_async_remote_copy(
            src_ref=ca_out.at[k], dst_ref=ca_in.at[mj], send_sem=ca_send.at[k], recv_sem=ca_recv.at[mj],
            device_id=group_peer(k), device_id_type=MESH)

    def send_carry(i, carry):
        k = lax.rem(mj + spread(i), nj)
        past = pre_v[k] + jnp.exp(-rate * (k * tokens).astype(F32)) * before
        ca_out[k] = (scaled * past).astype(ca_out.dtype)

        @pl.when(i < nj - 1)
        def _():
            carry_copy(k).start()

        return carry

    lax.fori_loop(0, nj, send_carry, 0)
    ca_in[mj] = ca_out[mj]

    lax.fori_loop(cut2, chunks, local_conv, 0)
    staged[6].wait()

    def finish_block(i, carry):
        b = lax.rem(mj + 2 * nj - spread(nj - 1 - i), nj)

        @pl.when(b != mj)
        def _():
            pltpu.make_async_remote_copy(
                src_ref=ca_out.at[b], dst_ref=ca_in.at[b], send_sem=ca_send.at[b], recv_sem=ca_recv.at[b],
                device_id=group_peer(b), device_id_type=MESH).wait_recv()

        lanes = pl.ds(pl.multiple_of(b * LANES, LANES), LANES)
        jump = rows_of(jnp.exp(-8.0 * rate_v[:, lanes]))
        weight = ca_in[b].astype(F32)
        terms = [pow_v[b * modes + m] * weight[m:m + 1, :] for m in range(modes)]
        for t in range(tokens // 16):
            first = total_of(terms)
            terms = [a * c for a, c in zip(terms, jump)]
            second = total_of(terms)
            if t < tokens // 16 - 1:
                terms = [a * c for a, c in zip(terms, jump)]
            both = jnp.concatenate([first, second], axis=0) + conv_v[t * 16:(t + 1) * 16, lanes]
            gate = gate_v[t * 16:(t + 1) * 16, lanes].astype(F32)
            out_ref[t * 16:(t + 1) * 16, lanes] = (both * gate).astype(BF16)
        return carry

    lax.fori_loop(0, blocks, finish_block, 0)

    for copy in sq_copies + tot_copies:
        copy.wait_send()

    def drain(k, carry):
        @pl.when(k != mj)
        def _():
            state_copy(k).wait_send()
            carry_copy(k).wait_send()

        return carry

    lax.fori_loop(0, nj, drain, 0)


def shards(nx, nseq, stream, norm_gain, gate_act, decay_rate, residue, skip_gain):
    tokens, chans = stream.shape
    modes = decay_rate.shape[1]
    blocks = chans // LANES
    nj = blocks
    ny = nseq // nj
    width = 256
    fwd, inv = half_tables(tokens)
    any_spec = pl.BlockSpec(memory_space=pl.ANY)
    vmem = pltpu.VMEM
    dma = pltpu.SemaphoreType.DMA
    return pl.pallas_call(
        functools.partial(kernel, nx, ny, nj, modes, width),
        out_shape=jax.ShapeDtypeStruct((tokens, chans), BF16),
        in_specs=[any_spec] * 8,
        out_specs=pl.BlockSpec(memory_space=pltpu.VMEM),
        scratch_shapes=[
            vmem((tokens, chans), BF16),
            vmem((tokens, chans), BF16),
            vmem((modes, chans), F32),
            vmem((modes, chans), F32),
            vmem((blocks, LANES), F32),
            vmem((blocks, LANES), F32),
            vmem(fwd.shape, BF16),
            vmem(inv.shape, BF16),
            vmem((tokens, LANES), F32),
            vmem((nx, 8, LANES), F32),
            vmem((tokens, LANES), F32),
            vmem((blocks * modes, 8, LANES), F32),
            vmem((2 * tokens, chans), BF16),
            vmem((tokens, chans), BF16),
            vmem((tokens, chans), F32),
            vmem((modes, LANES), F32),
            vmem((nj, modes, LANES), WIRE),
            vmem((nj, modes, LANES), WIRE),
            vmem((ny, modes, LANES), F32),
            vmem((nj, modes, LANES), F32),
            vmem((nj, modes, LANES), WIRE),
            vmem((nj, modes, LANES), WIRE),
            dma((7,)),
            dma((4,)),
            dma((nx,)),
            dma((nx,)),
            dma((nj,)),
            dma((nj,)),
            dma((ny,)),
            dma((ny,)),
            dma((nj,)),
            dma((nj,)),
        ],
        compiler_params=pltpu.CompilerParams(
            collective_id=0, has_side_effects=True, vmem_limit_bytes=32 * 1024 * 1024
        ),
    )(
        stream,
        decay_rate.T,
        residue.T,
        norm_gain.reshape(blocks, LANES),
        skip_gain.reshape(blocks, LANES),
        gate_act,
        jnp.asarray(fwd),
        jnp.asarray(inv),
    )


def solution(mesh):
    in_specs = (P("seq", "ch"), P("ch"), P("seq", "ch"), P("ch", None), P("ch", None), P("ch"))
    body = functools.partial(shards, mesh.shape["ch"], mesh.shape["seq"])
    return jax.shard_map(body, mesh=mesh, in_specs=in_specs, out_specs=P("seq", "ch"), check_vma=False)
```

profile of v0, /device:TPU:1, one launch (start us, length us, event | category | flops | bytes accessed | tf_op | source)
XLA Modules:
  0.0 36.6 jit_solution(12278968558035238971)
XLA Ops:
  0.0 0.0 copy-start
  0.0 1.0 %copy-done = bf16[128,2048]{1,0:T(8,128)(2,1)S(1)} copy-done((bf16[128,2048]{1,0:T(8,128)(2,1)S(1)}, bf16[128,2048]{1,0:T(8,128)(2,1)}, u32[]{:S(2)}) %copy-start) | copy-done | bytes 524312
  1.0 0.0 copy-start.1
  1.0 1.0 %copy-done.1 = bf16[128,2048]{1,0:T(8,128)(2,1)S(1)} copy-done((bf16[128,2048]{1,0:T(8,128)(2,1)S(1)}, bf16[128,2048]{1,0:T(8,128)(2,1)}, u32[]{:S(2)}) %copy-start.1) | copy-done | bytes 524312
  2.1 0.0 copy-start.2
  2.1 0.9 %copy-done.2 = f32[2048,16]{0,1:T(8,128)S(1)} copy-done((f32[2048,16]{0,1:T(8,128)S(1)}, f32[2048,16]{0,1:T(8,128)}, u32[]{:S(2)}) %copy-start.2) | copy-done | bytes 131096
  3.0 0.0 copy-start.3
  3.0 0.9 %copy-done.3 = f32[2048,16]{0,1:T(8,128)S(1)} copy-done((f32[2048,16]{0,1:T(8,128)S(1)}, f32[2048,16]{0,1:T(8,128)}, u32[]{:S(2)}) %copy-start.3) | copy-done | bytes 131096
  3.9 0.0 copy-start.4
  3.9 0.9 %copy-done.4 = bf16[128,512]{1,0:T(8,128)(2,1)S(1)} copy-done((bf16[128,512]{1,0:T(8,128)(2,1)S(1)}, bf16[128,512]{1,0:T(8,128)(2,1)}, u32[]{:S(2)}) %copy-start.4) | copy-done | bytes 131096
  4.8 0.0 copy-start.5
  4.8 0.9 %copy-done.5 = bf16[256,256]{1,0:T(8,128)(2,1)S(1)} copy-done((bf16[256,256]{1,0:T(8,128)(2,1)S(1)}, bf16[256,256]{1,0:T(8,128)(2,1)}, u32[]{:S(2)}) %copy-start.5) | copy-done | bytes 131096
  5.7 0.0 copy-start.6
  5.7 0.7 %copy-done.6 = f32[2048]{0:T(1024)S(1)} copy-done((f32[2048]{0:T(1024)S(1)}, f32[2048]{0:T(1024)}, u32[]{:S(2)}) %copy-start.6) | copy-done | bytes 8216
  6.4 0.0 copy-start.7
  6.4 0.7 %copy-done.7 = f32[2048]{0:T(1024)S(1)} copy-done((f32[2048]{0:T(1024)S(1)}, f32[2048]{0:T(1024)}, u32[]{:S(2)}) %copy-start.7) | copy-done | bytes 8216
  7.1 28.7 %shard_map.82 = bf16[128,2048]{1,0:T(8,128)(2,1)S(1)} custom-call(bf16[128,2048]{1,0:T(8,128)(2,1)S(1)} %copy-done, f32[16,2048]{1,0:T(8,128)S(1)} %bitcast.4, f32[16,2048]{1,0:T(8,128)S(1)} %bitcast.5, f32[16,128]{1,0:T(8,128)S(1)} %bitcast.6, f32[16,128]{1,0:T(8,128)S(1)} %bitcast.7, bf16[128,2048]{1,0:T(8,128)(2,1)S(1)} %copy-done.1, ...), custom_call_target="tpu_custom_call" | custom-call | tf_op jit(solution)/shard_map/pallas_call | solution.py:323
  35.8 0.8 %copy.10 = bf16[128,2048]{1,0:T(8,128)(2,1)} copy(bf16[128,2048]{1,0:T(8,128)(2,1)S(1)} %shard_map.82) | data formatting | bytes 1048576
Async XLA Ops:
  0.0 1.0 %copy-start = (bf16[128,2048]{1,0:T(8,128)(2,1)S(1)}, bf16[128,2048]{1,0:T(8,128)(2,1)}, u32[]{:S(2)}) copy-start(bf16[128,2048]{1,0:T(8,128)(2,1)} %x_hbm.1) | copy-start | bytes 1572868
  1.0 1.0 %copy-start.1 = (bf16[128,2048]{1,0:T(8,128)(2,1)S(1)}, bf16[128,2048]{1,0:T(8,128)(2,1)}, u32[]{:S(2)}) copy-start(bf16[128,2048]{1,0:T(8,128)(2,1)} %gate_hbm.1) | copy-start | bytes 1572868
  2.1 0.9 %copy-start.2 = (f32[2048,16]{0,1:T(8,128)S(1)}, f32[2048,16]{0,1:T(8,128)}, u32[]{:S(2)}) copy-start(f32[2048,16]{0,1:T(8,128)} %param.11) | copy-start | bytes 393220
  3.0 0.9 %copy-start.3 = (f32[2048,16]{0,1:T(8,128)S(1)}, f32[2048,16]{0,1:T(8,128)}, u32[]{:S(2)}) copy-start(f32[2048,16]{0,1:T(8,128)} %param.12) | copy-start | bytes 393220
  3.9 0.9 %copy-start.4 = (bf16[128,512]{1,0:T(8,128)(2,1)S(1)}, bf16[128,512]{1,0:T(8,128)(2,1)}, u32[]{:S(2)}) copy-start(bf16[128,512]{1,0:T(8,128)(2,1)} %constant.5.clone.inv_hbm) | copy-start | bytes 393220
  4.8 0.9 %copy-start.5 = (bf16[256,256]{1,0:T(8,128)(2,1)S(1)}, bf16[256,256]{1,0:T(8,128)(2,1)}, u32[]{:S(2)}) copy-start(bf16[256,256]{1,0:T(8,128)(2,1)} %constant.4.clone.fwd_hbm) | copy-start | bytes 393220
  5.7 0.7 %copy-start.6 = (f32[2048]{0:T(1024)S(1)}, f32[2048]{0:T(1024)}, u32[]{:S(2)}) copy-start(f32[2048]{0:T(1024)} %param.9) | copy-start | bytes 24580
  6.4 0.7 %copy-start.7 = (f32[2048]{0:T(1024)S(1)}, f32[2048]{0:T(1024)}, u32[]{:S(2)}) copy-start(f32[2048]{0:T(1024)} %param.13) | copy-start | bytes 24580
where the time goes:
time: 36.9 us; the launch traced here: 36.6 us
  Pallas kernels  28.7 us (78%)
  local copies, waits for them, and re-layouts  7.89 us (21%)
    pallas_call x1, Pallas kernels, shards(): pl.pallas_call(functools.partial(kernel, nx, ny, nj, modes, width), out_s...  28.7 us
    unnamed x17, local copies, waits for them, and re-layouts  7.89 us

commit v1 on v0

--- a/solution.py
+++ b/solution.py
@@ -360,9 +360,9 @@
             dma((nj,)),
         ],
         compiler_params=pltpu.CompilerParams(
-            collective_id=0, has_side_effects=True, vmem_limit_bytes=32 * 1024 * 1024
+            collective_id=0, has_side_effects=True, vmem_limit_bytes=40 * 1024 * 1024
         ),
-    )(
+    )(*[pltpu.with_memory_space_constraint(v, pltpu.HBM) for v in (
         stream,
         decay_rate.T,
         residue.T,
@@ -371,7 +371,7 @@
         gate_act,
         jnp.asarray(fwd),
         jnp.asarray(inv),
-    )
+    )])
 
 
 def solution(mesh):

time: 36.9 us -> 29.6 us (0.80)
  local copies, waits for them, and re-layouts: 7.89 us -> 0.8 us
    unnamed x17 -> x1, local copies, waits for them, and re-layouts: 7.89 us -> 0.8 us
where the time goes in v1:
time: 29.6 us; the launch traced here: 29.5 us
  Pallas kernels  28.7 us (97%)
  local copies, waits for them, and re-layouts  0.8 us (3%)
    pallas_call x1, Pallas kernels, shards(): pl.pallas_call(functools.partial(kernel, nx, ny, nj, modes, width), out_s...  28.7 us
    unnamed x1, local copies, waits for them, and re-layouts  0.8 us

profile of v1, /device:TPU:1, one launch (start us, length us, event | category | flops | bytes accessed | tf_op | source)
XLA Modules:
  0.0 29.5 jit_solution(14881712643113697666)
XLA Ops:
  0.0 28.7 %shard_map.82 = bf16[128,2048]{1,0:T(8,128)(2,1)S(1)} custom-call(bf16[128,2048]{1,0:T(8,128)(2,1)} %x_hbm.1, f32[16,2048]{1,0:T(8,128)} %bitcast.4, f32[16,2048]{1,0:T(8,128)} %bitcast.5, f32[16,128]{1,0:T(8,128)} %bitcast.6, f32[16,128]{1,0:T(8,128)} %bitcast.7, bf16[128,2048]{1,0:T(8,128)(2,1)} %gate_hbm.1, bf16[256,256]{1,0:T(8,128)(2,1)} %constant.4.clone.fwd_hbm, ...), custom_call_target="tpu_custom_call" | custom-call | tf_op jit(solution)/shard_map/pallas_call | solution.py:323
  28.8 0.8 %copy.10 = bf16[128,2048]{1,0:T(8,128)(2,1)} copy(bf16[128,2048]{1,0:T(8,128)(2,1)S(1)} %shard_map.82) | data formatting | bytes 1048576

commit v2 on v1

--- a/solution.py
+++ b/solution.py
@@ -13,6 +13,7 @@
 EPS = 1e-06
 LANES = 128
 WIRE = jnp.bfloat16
+CHIPS_Y = 4
 F32 = jnp.float32
 BF16 = jnp.bfloat16
 
@@ -46,33 +47,46 @@
     return items[0]
 
 
-def kernel(nx, ny, nj, modes, width,
+def kernel(nx, ny, nz, modes, width,
            x_hbm, rate_hbm, res_hbm, gain_hbm, skip_hbm, gate_hbm, fwd_hbm, inv_hbm, out_ref,
            x_v, gate_v, rate_v, res_v, gain_v, skip_v, fwd_v, inv_v,
-           sqacc_v, sq_v, scol_v, pow_v, taps_v, xn_v, conv_v, srow_v,
-           st_out, st_in, tot_v, pre_v, ca_out, ca_in,
-           in_sem, x_sem, sq_send, sq_recv, st_send, st_recv, tot_send, tot_recv, ca_send, ca_recv):
+           sqacc_v, sq_v, scol_v, pow_v, taps_v, xn_v, conv_v, srow_v, wa_v,
+           pair_out, pair_in, st_out, st_in, ca_out, ca_in,
+           in_sem, x_sem, sq_send, sq_recv, pair_send, pair_recv, st_send, st_recv, ca_send, ca_recv):
     tokens, chans = x_v.shape
     blocks = chans // LANES
+    nchips = ny * nz
+    half = modes // 2
     mx = lax.axis_index("ch")
     seq = lax.axis_index("seq")
-    my = seq // nj
-    mj = lax.rem(seq, nj)
-
-    def group_peer(k):
-        return {"seq": my * nj + k}
-
-    def spread(i):
-        half = nj // 2
-        return half + jnp.where(lax.rem(i, 2) == 1, (i + 1) // 2, -(i // 2))
+    chip = seq // 2
+    core = lax.rem(seq, 2)
+    my = chip // nz
+    mp = lax.rem(chip, nz) // 2
+
+    def chip_peer(q):
+        return {"seq": q * 2 + core}
+
+    partner = {"seq": chip * 2 + 1 - core}
+
+    def spread(n, i):
+        return n // 2 + jnp.where(lax.rem(i, 2) == 1, (i + 1) // 2, -(i // 2))
+
+    def block_of(i):
+        py = lax.rem(my + spread(ny, lax.rem(i, ny)), ny)
+        pz = lax.rem(mp + spread(nz // 2, i // ny), nz // 2)
+        return py * (nz // 2) + pz
 
     barrier = pltpu.get_barrier_semaphore()
     for d in range(1, nx):
         pl.semaphore_signal(barrier, inc=1, device_id={"ch": lax.rem(mx + d, nx)}, device_id_type=MESH)
-    for d in range(1, ny):
-        pl.semaphore_signal(barrier, inc=1, device_id={"seq": lax.rem(seq + d * nj, ny * nj)}, device_id_type=MESH)
-    for d in range(1, nj):
-        pl.semaphore_signal(barrier, inc=1, device_id=group_peer(lax.rem(mj + d, nj)), device_id_type=MESH)
+    pl.semaphore_signal(barrier, inc=1, device_id=partner, device_id_type=MESH)
+
+    def greet(d, carry):
+        pl.semaphore_signal(barrier, inc=1, device_id=chip_peer(lax.rem(chip + d, nchips)), device_id_type=MESH)
+        return carry
+
+    lax.fori_loop(1, nchips, greet, 0)
 
     parts = x_sem.shape[0]
     rows_part = tokens // parts
@@ -103,7 +117,7 @@
     turned = sqacc_v[...].T
     sq_v[mx] = total_of([turned[i * 8:(i + 1) * 8] for i in range(LANES // 8)])
 
-    pl.semaphore_wait(barrier, nx + ny + nj - 3)
+    pl.semaphore_wait(barrier, nx + nchips - 1)
     sq_copies = []
     for d in range(1, nx):
         copy = pltpu.make_async_remote_copy(
@@ -123,6 +137,7 @@
         lanes = pl.ds(pl.multiple_of(b * LANES, LANES), LANES)
         rate = rate_v[:, lanes]
         weight = res_v[:, lanes] * jnp.sqrt(one_minus_exp_neg(2.0 * rate))
+        wa_v[:, lanes] = weight * jnp.exp(-rate)
         jump = rows_of(jnp.exp(-8.0 * rate))
         terms = []
         for m in range(modes):
@@ -152,13 +167,16 @@
     scale = lax.rsqrt(squares / (nx * chans) + EPS)
     scol_v[...] = jnp.broadcast_to(scale, (tokens, LANES)).T
 
-    def state_copy(b):
+    batch = blocks // pair_send.shape[0]
+
+    def pair_copy(g):
+        slots = pl.ds(g * batch, batch)
         return pltpu.make_async_remote_copy(
-            src_ref=st_out.at[b], dst_ref=st_in.at[mj], send_sem=st_send.at[b], recv_sem=st_recv.at[mj],
-            device_id=group_peer(b), device_id_type=MESH)
+            src_ref=pair_out.at[slots], dst_ref=pair_in.at[slots], send_sem=pair_send.at[g], recv_sem=pair_recv.at[g],
+            device_id=partner, device_id_type=MESH)
 
     def state_block(i, carry):
-        b = lax.rem(mj + spread(i), nj)
+        b = block_of(i)
         lanes = pl.ds(pl.multiple_of(b * LANES, LANES), LANES)
         rate = rate_v[:, lanes]
         jump = rows_of(jnp.exp(-8.0 * rate))
@@ -174,16 +192,41 @@
         for m in range(modes):
             left = jnp.exp(-rate[m:m + 1, :] * (7.0 - step8))
             srow_v[m:m + 1, :] = jnp.sum(sums[m] * left, axis=0, keepdims=True)
-        st_out[b] = srow_v[...].astype(st_out.dtype)
-
-        @pl.when(i < nj - 1)
+        pair_out[i] = srow_v[...]
+
+        @pl.when(lax.rem(i, batch) == batch - 1)
         def _():
-            state_copy(b).start()
-
-        return carry
-
-    lax.fori_loop(0, nj, state_block, 0)
-    st_in[mj] = st_out[mj]
+            pair_copy(i // batch).start()
+
+        return carry
+
+    lax.fori_loop(0, blocks, state_block, 0)
+
+    def state_copy(q):
+        return pltpu.make_async_remote_copy(
+            src_ref=st_out.at[q], dst_ref=st_in.at[chip], send_sem=st_send.at[q], recv_sem=st_recv.at[chip],
+            device_id=chip_peer(q), device_id_type=MESH)
+
+    def join_block(i, carry):
+        @pl.when(lax.rem(i, batch) == 0)
+        def _():
+            pair_copy(i // batch).wait_recv()
+
+        b = block_of(i)
+        decay = jnp.exp(-float(tokens) * rate_v[:, pl.ds(pl.multiple_of(b * LANES, LANES), LANES)])
+        mine, other = pair_out[i], pair_in[i]
+        joined = jnp.where(core == 0, mine * decay + other, other * decay + mine)
+        st_out[2 * b] = joined[:half].astype(st_out.dtype)
+        st_out[2 * b + 1] = joined[half:].astype(st_out.dtype)
+        for n in range(2):
+            @pl.when(2 * b + n != chip)
+            def _():
+                state_copy(2 * b + n).start()
+
+        return carry
+
+    lax.fori_loop(0, blocks, join_block, 0)
+    st_in[chip] = st_out[chip]
 
     def local_conv(c, carry):
         lanes = pl.ds(pl.multiple_of(c * width, width), width)
@@ -206,81 +249,63 @@
         return carry
 
     chunks = chans // width
-    cut1, cut2 = chunks // 2, (3 * chunks) // 4
+    cut1 = chunks // 2
     lax.fori_loop(0, cut1, local_conv, 0)
 
-    own = pl.ds(pl.multiple_of(mj * LANES, LANES), LANES)
-    rate = rate_v[:, own]
-    decay = jnp.exp(-float(tokens) * rate)
-
-    def scan_group(k, state):
-        @pl.when(k != mj)
+    own = pl.ds(pl.multiple_of((chip // 2) * LANES, LANES), LANES)
+    rate = rate_v[pl.ds(pl.multiple_of(lax.rem(chip, 2) * half, half), half), own]
+    decay = jnp.exp(-float(2 * tokens) * rate)
+
+    def scan_chips(q, state):
+        @pl.when(q != chip)
         def _():
             pltpu.make_async_remote_copy(
-                src_ref=st_out.at[k], dst_ref=st_in.at[k], send_sem=st_send.at[k], recv_sem=st_recv.at[k],
-                device_id=group_peer(k), device_id_type=MESH).wait_recv()
-
-        pre_v[k] = state
-        return state * decay + st_in[k].astype(F32)
-
-    tot_v[my] = lax.fori_loop(0, nj, scan_group, jnp.zeros((modes, LANES), F32))
-
-    tot_copies = []
-    for d in range(1, ny):
-        copy = pltpu.make_async_remote_copy(
-            src_ref=tot_v.at[my], dst_ref=tot_v.at[my], send_sem=tot_send.at[d], recv_sem=tot_recv.at[my],
-            device_id={"seq": lax.rem(seq + d * nj, ny * nj)}, device_id_type=MESH)
-        copy.start()
-        tot_copies.append(copy)
-
-    lax.fori_loop(cut1, cut2, local_conv, 0)
-
-    for d in range(1, ny):
-        src = lax.rem(my + d, ny)
-        pltpu.make_async_remote_copy(
-            src_ref=tot_v.at[src], dst_ref=tot_v.at[src], send_sem=tot_send.at[d], recv_sem=tot_recv.at[src],
-            device_id={"seq": src * nj + mj}, device_id_type=MESH).wait_recv()
-    before = jnp.zeros((modes, LANES), F32)
-    for k in range(ny):
-        steps = jnp.maximum(my - 1 - k, 0) * (nj * tokens)
-        live = (k < my).astype(F32)
-        before = before + live * jnp.exp(-rate * steps.astype(F32)) * tot_v[k]
-    scaled = res_v[:, own] * jnp.sqrt(one_minus_exp_neg(2.0 * rate)) * jnp.exp(-rate)
-
-    def carry_copy(k):
+                src_ref=st_out.at[q], dst_ref=st_in.at[q], send_sem=st_send.at[q], recv_sem=st_recv.at[q],
+                device_id=chip_peer(q), device_id_type=MESH).wait_recv()
+
+        ca_out[q] = state.astype(ca_out.dtype)
+        return state * decay + st_in[q].astype(F32)
+
+    lax.fori_loop(0, nchips, scan_chips, jnp.zeros((half, LANES), F32))
+
+    def carry_copy(q):
         return pltpu.make_async_remote_copy(
-            src_ref=ca_out.at[k], dst_ref=ca_in.at[mj], send_sem=ca_send.at[k], recv_sem=ca_recv.at[mj],
-            device_id=group_peer(k), device_id_type=MESH)
+            src_ref=ca_out.at[q], dst_ref=ca_in.at[chip], send_sem=ca_send.at[q], recv_sem=ca_recv.at[chip],
+            device_id=chip_peer(q), device_id_type=MESH)
 
     def send_carry(i, carry):
-        k = lax.rem(mj + spread(i), nj)
-        past = pre_v[k] + jnp.exp(-rate * (k * tokens).astype(F32)) * before
-        ca_out[k] = (scaled * past).astype(ca_out.dtype)
-
-        @pl.when(i < nj - 1)
+        q = lax.rem(i, ny) * nz + i // ny
+
+        @pl.when(q != chip)
         def _():
-            carry_copy(k).start()
-
-        return carry
-
-    lax.fori_loop(0, nj, send_carry, 0)
-    ca_in[mj] = ca_out[mj]
-
-    lax.fori_loop(cut2, chunks, local_conv, 0)
+            carry_copy(q).start()
+
+        return carry
+
+    lax.fori_loop(0, nchips, send_carry, 0)
+    ca_in[chip] = ca_out[chip]
+
+    lax.fori_loop(cut1, chunks, local_conv, 0)
     staged[6].wait()
 
     def finish_block(i, carry):
-        b = lax.rem(mj + 2 * nj - spread(nj - 1 - i), nj)
-
-        @pl.when(b != mj)
-        def _():
-            pltpu.make_async_remote_copy(
-                src_ref=ca_out.at[b], dst_ref=ca_in.at[b], send_sem=ca_send.at[b], recv_sem=ca_recv.at[b],
-                device_id=group_peer(b), device_id_type=MESH).wait_recv()
+        slot = blocks - 1 - i
+        b = block_of(slot)
+        for n in range(2):
+            q = 2 * b + n
+
+            @pl.when(q != chip)
+            def _():
+                pltpu.make_async_remote_copy(
+                    src_ref=ca_out.at[q], dst_ref=ca_in.at[q], send_sem=ca_send.at[q], recv_sem=ca_recv.at[q],
+                    device_id=chip_peer(q), device_id_type=MESH).wait_recv()
 
         lanes = pl.ds(pl.multiple_of(b * LANES, LANES), LANES)
-        jump = rows_of(jnp.exp(-8.0 * rate_v[:, lanes]))
-        weight = ca_in[b].astype(F32)
+        rate = rate_v[:, lanes]
+        jump = rows_of(jnp.exp(-8.0 * rate))
+        past = jnp.concatenate([ca_in[2 * b].astype(F32), ca_in[2 * b + 1].astype(F32)], axis=0)
+        past = jnp.where(core == 0, past, past * jnp.exp(-float(tokens) * rate) + pair_in[slot])
+        weight = past * wa_v[:, lanes]
         terms = [pow_v[b * modes + m] * weight[m:m + 1, :] for m in range(modes)]
         for t in range(tokens // 16):
             first = total_of(terms)
@@ -295,33 +320,37 @@
 
     lax.fori_loop(0, blocks, finish_block, 0)
 
-    for copy in sq_copies + tot_copies:
+    for copy in sq_copies:
         copy.wait_send()
-
-    def drain(k, carry):
-        @pl.when(k != mj)
+    for g in range(pair_send.shape[0]):
+        pair_copy(g).wait_send()
+
+    def drain(q, carry):
+        @pl.when(q != chip)
         def _():
-            state_copy(k).wait_send()
-            carry_copy(k).wait_send()
-
-        return carry
-
-    lax.fori_loop(0, nj, drain, 0)
+            state_copy(q).wait_send()
+            carry_copy(q).wait_send()
+
+        return carry
+
+    lax.fori_loop(0, nchips, drain, 0)
 
 
 def shards(nx, nseq, stream, norm_gain, gate_act, decay_rate, residue, skip_gain):
     tokens, chans = stream.shape
     modes = decay_rate.shape[1]
     blocks = chans // LANES
-    nj = blocks
-    ny = nseq // nj
+    nchips = nseq // 2
+    ny = CHIPS_Y
+    nz = nchips // ny
     width = 256
+    pairs = min(4, blocks)
     fwd, inv = half_tables(tokens)
     any_spec = pl.BlockSpec(memory_space=pl.ANY)
     vmem = pltpu.VMEM
     dma = pltpu.SemaphoreType.DMA
     return pl.pallas_call(
-        functools.partial(kernel, nx, ny, nj, modes, width),
+        functools.partial(kernel, nx, ny, nz, modes, width),
         out_shape=jax.ShapeDtypeStruct((tokens, chans), BF16),
         in_specs=[any_spec] * 8,
         out_specs=pl.BlockSpec(memory_space=pltpu.VMEM),
@@ -342,22 +371,23 @@
             vmem((tokens, chans), BF16),
             vmem((tokens, chans), F32),
             vmem((modes, LANES), F32),
-            vmem((nj, modes, LANES), WIRE),
-            vmem((nj, modes, LANES), WIRE),
-            vmem((ny, modes, LANES), F32),
-            vmem((nj, modes, LANES), F32),
-            vmem((nj, modes, LANES), WIRE),
-            vmem((nj, modes, LANES), WIRE),
+            vmem((modes, chans), F32),
+            vmem((blocks, modes, LANES), F32),
+            vmem((blocks, modes, LANES), F32),
+            vmem((nchips, modes // 2, LANES), WIRE),
+            vmem((nchips, modes // 2, LANES), WIRE),
+            vmem((nchips, modes // 2, LANES), WIRE),
+            vmem((nchips, modes // 2, LANES), WIRE),
             dma((7,)),
             dma((4,)),
             dma((nx,)),
             dma((nx,)),
-            dma((nj,)),
-            dma((nj,)),
-            dma((ny,)),
-            dma((ny,)),
-            dma((nj,)),
-            dma((nj,)),
+            dma((pairs,)),
+            dma((pairs,)),
+            dma((nchips,)),
+            dma((nchips,)),
+            dma((nchips,)),
+            dma((nchips,)),
         ],
         compiler_params=pltpu.CompilerParams(
             collective_id=0, has_side_effects=True, vmem_limit_bytes=40 * 1024 * 1024

time: 29.6 us -> 30.9 us (1.044)
  Pallas kernels: 28.7 us -> 29.9 us
    pallas_call x1, Pallas kernels: 28.7 us -> 29.9 us  [shards(): pl.pallas_call(functools.partial(kernel, nx, ny, nz, modes, width), out_s...]
where the time goes in v2:
time: 30.9 us; the launch traced here: 30.7 us
  Pallas kernels  29.9 us (97%)
  local copies, waits for them, and re-layouts  0.8 us (3%)
    pallas_call x1, Pallas kernels, shards(): pl.pallas_call(functools.partial(kernel, nx, ny, nz, modes, width), out_s...  29.9 us
    unnamed x1, local copies, waits for them, and re-layouts  0.8 us

profile of v2, /device:TPU:1, one launch (start us, length us, event | category | flops | bytes accessed | tf_op | source)
XLA Modules:
  0.0 30.7 jit_solution(11609936316742809396)
XLA Ops:
  0.0 29.9 %shard_map.82 = bf16[128,2048]{1,0:T(8,128)(2,1)S(1)} custom-call(bf16[128,2048]{1,0:T(8,128)(2,1)} %x_hbm.1, f32[16,2048]{1,0:T(8,128)} %bitcast.4, f32[16,2048]{1,0:T(8,128)} %bitcast.5, f32[16,128]{1,0:T(8,128)} %bitcast.6, f32[16,128]{1,0:T(8,128)} %bitcast.7, bf16[128,2048]{1,0:T(8,128)(2,1)} %gate_hbm.1, bf16[256,256]{1,0:T(8,128)(2,1)} %constant.4.clone.fwd_hbm, ...), custom_call_target="tpu_custom_call" | custom-call | tf_op jit(solution)/shard_map/pallas_call | solution.py:352
  29.9 0.8 %copy.10 = bf16[128,2048]{1,0:T(8,128)(2,1)} copy(bf16[128,2048]{1,0:T(8,128)(2,1)S(1)} %shard_map.82) | data formatting | bytes 1048576

commit v3 on v1

--- a/solution.py
+++ b/solution.py
@@ -46,10 +46,24 @@
     return items[0]
 
 
+def rows_of(tile):
+    return [jnp.broadcast_to(tile[m:m + 1, :], (8, LANES)) for m in range(tile.shape[0])]
+
+
+def row_sums(tiles):
+    row = lax.broadcasted_iota(jnp.int32, (8, LANES), 0)
+    for bit in (4, 2, 1):
+        clear = lax.rem(row // bit, 2) == 0
+        count = len(tiles) // 2
+        tiles = [jnp.where(clear, a + pltpu.roll(a, 8 - bit, 0), c + pltpu.roll(c, bit, 0))
+                 for a, c in zip(tiles[:count], tiles[count:])]
+    return tiles[0]
+
+
 def kernel(nx, ny, nj, modes, width,
            x_hbm, rate_hbm, res_hbm, gain_hbm, skip_hbm, gate_hbm, fwd_hbm, inv_hbm, out_ref,
            x_v, gate_v, rate_v, res_v, gain_v, skip_v, fwd_v, inv_v,
-           sqacc_v, sq_v, scol_v, pow_v, taps_v, xn_v, conv_v, srow_v,
+           sqacc_v, sq_v, scol_v, pow_v, taps_v, xn_v, conv_v, left_v, jump_v,
            st_out, st_in, tot_v, pre_v, ca_out, ca_in,
            in_sem, x_sem, sq_send, sq_recv, st_send, st_recv, tot_send, tot_recv, ca_send, ca_recv):
     tokens, chans = x_v.shape
@@ -63,16 +77,7 @@
         return {"seq": my * nj + k}
 
     def spread(i):
-        half = nj // 2
-        return half + jnp.where(lax.rem(i, 2) == 1, (i + 1) // 2, -(i // 2))
-
-    barrier = pltpu.get_barrier_semaphore()
-    for d in range(1, nx):
-        pl.semaphore_signal(barrier, inc=1, device_id={"ch": lax.rem(mx + d, nx)}, device_id_type=MESH)
-    for d in range(1, ny):
-        pl.semaphore_signal(barrier, inc=1, device_id={"seq": lax.rem(seq + d * nj, ny * nj)}, device_id_type=MESH)
-    for d in range(1, nj):
-        pl.semaphore_signal(barrier, inc=1, device_id=group_peer(lax.rem(mj + d, nj)), device_id_type=MESH)
+        return nj // 2 + jnp.where(lax.rem(i, 2) == 1, (i + 1) // 2, -(i // 2))
 
     parts = x_sem.shape[0]
     rows_part = tokens // parts
@@ -85,6 +90,24 @@
     for copy in staged:
         copy.start()
 
+    half = nj // 2
+    late = mj >= half
+    barrier = pltpu.get_barrier_semaphore()
+    for d in range(1, nx):
+        pl.semaphore_signal(barrier, inc=1, device_id={"ch": lax.rem(mx + d, nx)}, device_id_type=MESH)
+    for d in range(1, ny):
+        pl.semaphore_signal(barrier, inc=1, device_id={"seq": lax.rem(seq + d * nj, ny * nj)}, device_id_type=MESH)
+
+    def greet(first):
+        for k in range(first, first + half):
+            @pl.when(k != mj)
+            def _():
+                pl.semaphore_signal(barrier, inc=1, device_id=group_peer(k), device_id_type=MESH)
+
+    @pl.when(late)
+    def _():
+        greet(half)
+
     tiles_part = rows_part // 16
     for p in range(parts):
         rows = pl.ds(p * rows_part, rows_part)
@@ -103,7 +126,16 @@
     turned = sqacc_v[...].T
     sq_v[mx] = total_of([turned[i * 8:(i + 1) * 8] for i in range(LANES // 8)])
 
-    pl.semaphore_wait(barrier, nx + ny + nj - 3)
+    @pl.when(late)
+    def _():
+        pl.semaphore_wait(barrier, nx + ny + nj - 3)
+        greet(0)
+
+    @pl.when(jnp.logical_not(late))
+    def _():
+        pl.semaphore_wait(barrier, nx + ny - 2)
+        greet(half)
+
     sq_copies = []
     for d in range(1, nx):
         copy = pltpu.make_async_remote_copy(
@@ -116,18 +148,18 @@
         copy.wait()
     step8 = lax.broadcasted_iota(jnp.int32, (8, LANES), 0).astype(F32)
 
-    def rows_of(tile):
-        return [jnp.broadcast_to(tile[m:m + 1, :], (8, LANES)) for m in range(modes)]
-
     def filter_block(b, carry):
         lanes = pl.ds(pl.multiple_of(b * LANES, LANES), LANES)
         rate = rate_v[:, lanes]
         weight = res_v[:, lanes] * jnp.sqrt(one_minus_exp_neg(2.0 * rate))
-        jump = rows_of(jnp.exp(-8.0 * rate))
+        jump = jnp.exp(-8.0 * rate)
+        jump_v[:, lanes] = jump
+        jump = rows_of(jump)
         terms = []
         for m in range(modes):
             power = jnp.exp(-rate[m:m + 1, :] * step8)
             pow_v[b * modes + m] = power
+            left_v[b * modes + m] = jnp.exp(-rate[m:m + 1, :] * (7.0 - step8))
             terms.append(power * weight[m:m + 1, :])
         for t in range(tokens // 16):
             first = total_of(terms)
@@ -160,8 +192,7 @@
     def state_block(i, carry):
         b = lax.rem(mj + spread(i), nj)
         lanes = pl.ds(pl.multiple_of(b * LANES, LANES), LANES)
-        rate = rate_v[:, lanes]
-        jump = rows_of(jnp.exp(-8.0 * rate))
+        jump = rows_of(jump_v[:, lanes])
         gain = gain_v[pl.ds(b, 1), :]
         sums = [None] * modes
         for t in range(tokens // 16):
@@ -171,12 +202,11 @@
             value = value.astype(F32)
             for part in (value[:8], value[8:]):
                 sums = [part if s is None else s * c + part for s, c in zip(sums, jump)]
-        for m in range(modes):
-            left = jnp.exp(-rate[m:m + 1, :] * (7.0 - step8))
-            srow_v[m:m + 1, :] = jnp.sum(sums[m] * left, axis=0, keepdims=True)
-        st_out[b] = srow_v[...].astype(st_out.dtype)
-
-        @pl.when(i < nj - 1)
+        sums = [s * left_v[b * modes + m] for m, s in enumerate(sums)]
+        sums = jnp.concatenate([row_sums(sums[n:n + 8]) for n in range(0, modes, 8)], axis=0)
+        st_out[b] = sums.astype(st_out.dtype)
+
+        @pl.when(late & (i < nj - 1))
         def _():
             state_copy(b).start()
 
@@ -184,6 +214,16 @@
 
     lax.fori_loop(0, nj, state_block, 0)
     st_in[mj] = st_out[mj]
+
+    @pl.when(jnp.logical_not(late))
+    def _():
+        pl.semaphore_wait(barrier, nj // 2)
+
+        def send_state(i, carry):
+            state_copy(lax.rem(mj + spread(i), nj)).start()
+            return carry
+
+        lax.fori_loop(0, nj - 1, send_state, 0)
 
     def local_conv(c, carry):
         lanes = pl.ds(pl.multiple_of(c * width, width), width)
@@ -279,7 +319,7 @@
                 device_id=group_peer(b), device_id_type=MESH).wait_recv()
 
         lanes = pl.ds(pl.multiple_of(b * LANES, LANES), LANES)
-        jump = rows_of(jnp.exp(-8.0 * rate_v[:, lanes]))
+        jump = rows_of(jump_v[:, lanes])
         weight = ca_in[b].astype(F32)
         terms = [pow_v[b * modes + m] * weight[m:m + 1, :] for m in range(modes)]
         for t in range(tokens // 16):
@@ -341,7 +381,8 @@
             vmem((2 * tokens, chans), BF16),
             vmem((tokens, chans), BF16),
             vmem((tokens, chans), F32),
-            vmem((modes, LANES), F32),
+            vmem((blocks * modes, 8, LANES), F32),
+            vmem((modes, chans), F32),
             vmem((nj, modes, LANES), WIRE),
             vmem((nj, modes, LANES), WIRE),
             vmem((ny, modes, LANES), F32),

time: 29.6 us -> 28.9 us (0.976)
  Pallas kernels: 28.7 us -> 28 us
    pallas_call x1, Pallas kernels: 28.7 us -> 28 us  [shards(): pl.pallas_call(functools.partial(kernel, nx, ny, nj, modes, width), out_s...]
where the time goes in v3:
time: 28.9 us
  Pallas kernels  28 us (97%)
  local copies, waits for them, and re-layouts  0.8 us (3%)
    pallas_call x1, Pallas kernels, shards(): pl.pallas_call(functools.partial(kernel, nx, ny, nj, modes, width), out_s...  28 us
    unnamed x1, local copies, waits for them, and re-layouts  0.8 us

profile of v3, /device:TPU:1, one launch (start us, length us, event | category | flops | bytes accessed | tf_op | source)
XLA Modules:
  0.0 28.9 jit_solution(6442910312263453902)
XLA Ops:
  0.0 28.0 %shard_map.82 = bf16[128,2048]{1,0:T(8,128)(2,1)S(1)} custom-call(bf16[128,2048]{1,0:T(8,128)(2,1)} %x_hbm.1, f32[16,2048]{1,0:T(8,128)} %bitcast.4, f32[16,2048]{1,0:T(8,128)} %bitcast.5, f32[16,128]{1,0:T(8,128)} %bitcast.6, f32[16,128]{1,0:T(8,128)} %bitcast.7, bf16[128,2048]{1,0:T(8,128)(2,1)} %gate_hbm.1, bf16[256,256]{1,0:T(8,128)(2,1)} %constant.4.clone.fwd_hbm, ...), custom_call_target="tpu_custom_call" | custom-call | tf_op jit(solution)/shard_map/pallas_call | solution.py:363
  28.1 0.8 %copy.10 = bf16[128,2048]{1,0:T(8,128)(2,1)} copy(bf16[128,2048]{1,0:T(8,128)(2,1)S(1)} %shard_map.82) | data formatting | bytes 1048576

commit v4 on v3

--- a/solution.py
+++ b/solution.py
@@ -63,8 +63,8 @@
 def kernel(nx, ny, nj, modes, width,
            x_hbm, rate_hbm, res_hbm, gain_hbm, skip_hbm, gate_hbm, fwd_hbm, inv_hbm, out_ref,
            x_v, gate_v, rate_v, res_v, gain_v, skip_v, fwd_v, inv_v,
-           sqacc_v, sq_v, scol_v, pow_v, taps_v, xn_v, conv_v, left_v, jump_v,
-           st_out, st_in, tot_v, pre_v, ca_out, ca_in,
+           sqacc_v, sq_v, scol_v, pow_v, taps_v, conv_v, left_v, jump_v,
+           st_out, st_in, tot_v, before_v, pre_v, fac_v, ca_out, ca_in,
            in_sem, x_sem, sq_send, sq_recv, st_send, st_recv, tot_send, tot_recv, ca_send, ca_recv):
     tokens, chans = x_v.shape
     blocks = chans // LANES
@@ -189,30 +189,34 @@
             src_ref=st_out.at[b], dst_ref=st_in.at[mj], send_sem=st_send.at[b], recv_sem=st_recv.at[mj],
             device_id=group_peer(b), device_id_type=MESH)
 
-    def state_block(i, carry):
-        b = lax.rem(mj + spread(i), nj)
+    def state_of(b):
         lanes = pl.ds(pl.multiple_of(b * LANES, LANES), LANES)
         jump = rows_of(jump_v[:, lanes])
-        gain = gain_v[pl.ds(b, 1), :]
         sums = [None] * modes
         for t in range(tokens // 16):
-            value = x_v[t * 16:(t + 1) * 16, lanes].astype(F32) * scol_v[t * 16:(t + 1) * 16, :] * gain
-            value = value.astype(BF16)
-            xn_v[t * 16:(t + 1) * 16, lanes] = value
-            value = value.astype(F32)
+            value = x_v[t * 16:(t + 1) * 16, lanes].astype(F32) * scol_v[t * 16:(t + 1) * 16, :]
             for part in (value[:8], value[8:]):
                 sums = [part if s is None else s * c + part for s, c in zip(sums, jump)]
         sums = [s * left_v[b * modes + m] for m, s in enumerate(sums)]
         sums = jnp.concatenate([row_sums(sums[n:n + 8]) for n in range(0, modes, 8)], axis=0)
-        st_out[b] = sums.astype(st_out.dtype)
-
-        @pl.when(late & (i < nj - 1))
-        def _():
-            state_copy(b).start()
-
-        return carry
-
-    lax.fori_loop(0, nj, state_block, 0)
+        st_out[b] = (sums * gain_v[pl.ds(b, 1), :]).astype(st_out.dtype)
+
+    def state_blocks(i, carry):
+        pair = [lax.rem(mj + spread(2 * i + n), nj) for n in range(2)]
+        for b in pair:
+            state_of(b)
+
+        @pl.when(late)
+        def _():
+            state_copy(pair[0]).start()
+
+            @pl.when(i < nj // 2 - 1)
+            def _():
+                state_copy(pair[1]).start()
+
+        return carry
+
+    lax.fori_loop(0, nj // 2, state_blocks, 0)
     st_in[mj] = st_out[mj]
 
     @pl.when(jnp.logical_not(late))
@@ -227,7 +231,10 @@
 
     def local_conv(c, carry):
         lanes = pl.ds(pl.multiple_of(c * width, width), width)
-        xn = xn_v[:, lanes]
+        per = width // LANES
+        scale = jnp.concatenate([scol_v[...]] * per, axis=1)
+        gain = jnp.concatenate([gain_v[pl.ds(c * per + n, 1), :] for n in range(per)], axis=1)
+        xn = (x_v[:, lanes].astype(F32) * scale * gain).astype(BF16)
         high = taps_v[:tokens, lanes]
         low = taps_v[tokens:, lanes]
         spec = jnp.dot(fwd_v[...], jnp.concatenate([xn, xn], axis=0), preferred_element_type=F32)
@@ -240,7 +247,6 @@
         plow = (prod - phigh.astype(F32)).astype(BF16)
         conv = jnp.dot(inv_v[...], jnp.concatenate([phigh, phigh], axis=0), preferred_element_type=F32)
         conv = conv + jnp.dot(inv_v[:, :2 * tokens], plow, preferred_element_type=F32)
-        per = width // LANES
         skip = jnp.concatenate([skip_v[pl.ds(c * per + n, 1), :] for n in range(per)], axis=1)
         conv_v[:, lanes] = conv + skip * xn.astype(F32)
         return carry
@@ -265,27 +271,40 @@
 
     tot_v[my] = lax.fori_loop(0, nj, scan_group, jnp.zeros((modes, LANES), F32))
 
-    tot_copies = []
-    for d in range(1, ny):
-        copy = pltpu.make_async_remote_copy(
+    def total_copy(d):
+        return pltpu.make_async_remote_copy(
             src_ref=tot_v.at[my], dst_ref=tot_v.at[my], send_sem=tot_send.at[d], recv_sem=tot_recv.at[my],
             device_id={"seq": lax.rem(seq + d * nj, ny * nj)}, device_id_type=MESH)
-        copy.start()
-        tot_copies.append(copy)
+
+    for d in range(1, ny):
+        @pl.when(my + d < ny)
+        def _():
+            total_copy(d).start()
 
     lax.fori_loop(cut1, cut2, local_conv, 0)
 
-    for d in range(1, ny):
-        src = lax.rem(my + d, ny)
-        pltpu.make_async_remote_copy(
-            src_ref=tot_v.at[src], dst_ref=tot_v.at[src], send_sem=tot_send.at[d], recv_sem=tot_recv.at[src],
-            device_id={"seq": src * nj + mj}, device_id_type=MESH).wait_recv()
-    before = jnp.zeros((modes, LANES), F32)
-    for k in range(ny):
+    scaled = res_v[:, own] * jnp.sqrt(one_minus_exp_neg(2.0 * rate)) * jnp.exp(-rate)
+    shares = []
+    for k in range(ny - 1):
         steps = jnp.maximum(my - 1 - k, 0) * (nj * tokens)
-        live = (k < my).astype(F32)
-        before = before + live * jnp.exp(-rate * steps.astype(F32)) * tot_v[k]
-    scaled = res_v[:, own] * jnp.sqrt(one_minus_exp_neg(2.0 * rate)) * jnp.exp(-rate)
+        shares.append(jnp.exp(-rate * steps.astype(F32)))
+
+    def factors(k, carry):
+        pre_v[k] = scaled * pre_v[k]
+        fac_v[k] = scaled * jnp.exp(-rate * (k * tokens).astype(F32))
+        return carry
+
+    lax.fori_loop(0, nj, factors, 0)
+    before_v[...] = jnp.zeros((modes, LANES), F32)
+    for k in range(ny - 1):
+        @pl.when(k < my)
+        def _():
+            pltpu.make_async_remote_copy(
+                src_ref=tot_v.at[k], dst_ref=tot_v.at[k], send_sem=tot_send.at[1], recv_sem=tot_recv.at[k],
+                device_id={"seq": k * nj + mj}, device_id_type=MESH).wait_recv()
+            before_v[...] += shares[k] * tot_v[k]
+
+    before = before_v[...]
 
     def carry_copy(k):
         return pltpu.make_async_remote_copy(
@@ -294,8 +313,7 @@
 
     def send_carry(i, carry):
         k = lax.rem(mj + spread(i), nj)
-        past = pre_v[k] + jnp.exp(-rate * (k * tokens).astype(F32)) * before
-        ca_out[k] = (scaled * past).astype(ca_out.dtype)
+        ca_out[k] = (pre_v[k] + fac_v[k] * before).astype(ca_out.dtype)
 
         @pl.when(i < nj - 1)
         def _():
@@ -308,6 +326,21 @@
 
     lax.fori_loop(cut2, chunks, local_conv, 0)
     staged[6].wait()
+    for copy in sq_copies:
+        copy.wait_send()
+    for d in range(1, ny):
+        @pl.when(my + d < ny)
+        def _():
+            total_copy(d).wait_send()
+
+    def drain_states(k, carry):
+        @pl.when(k != mj)
+        def _():
+            state_copy(k).wait_send()
+
+        return carry
+
+    lax.fori_loop(0, nj, drain_states, 0)
 
     def finish_block(i, carry):
         b = lax.rem(mj + 2 * nj - spread(nj - 1 - i), nj)
@@ -333,20 +366,16 @@
             out_ref[t * 16:(t + 1) * 16, lanes] = (both * gate).astype(BF16)
         return carry
 
-    lax.fori_loop(0, blocks, finish_block, 0)
-
-    for copy in sq_copies + tot_copies:
-        copy.wait_send()
-
-    def drain(k, carry):
+    def drain_carries(k, carry):
         @pl.when(k != mj)
         def _():
-            state_copy(k).wait_send()
             carry_copy(k).wait_send()
 
         return carry
 
-    lax.fori_loop(0, nj, drain, 0)
+    lax.fori_loop(0, blocks // 4, finish_block, 0)
+    lax.fori_loop(0, nj, drain_carries, 0)
+    lax.fori_loop(blocks // 4, blocks, finish_block, 0)
 
 
 def shards(nx, nseq, stream, norm_gain, gate_act, decay_rate, residue, skip_gain):
@@ -379,13 +408,14 @@
             vmem((tokens, LANES), F32),
             vmem((blocks * modes, 8, LANES), F32),
             vmem((2 * tokens, chans), BF16),
-            vmem((tokens, chans), BF16),
             vmem((tokens, chans), F32),
             vmem((blocks * modes, 8, LANES), F32),
             vmem((modes, chans), F32),
             vmem((nj, modes, LANES), WIRE),
             vmem((nj, modes, LANES), WIRE),
             vmem((ny, modes, LANES), F32),
+            vmem((modes, LANES), F32),
+            vmem((nj, modes, LANES), F32),
             vmem((nj, modes, LANES), F32),
             vmem((nj, modes, LANES), WIRE),
             vmem((nj, modes, LANES), WIRE),

time: 28.9 us -> 27 us (0.934)
  Pallas kernels: 28 us -> 26.1 us
    pallas_call x1, Pallas kernels: 28 us -> 26.1 us  [shards(): pl.pallas_call(functools.partial(kernel, nx, ny, nj, modes, width), out_s...]
where the time goes in v4:
time: 27 us; the launch traced here: 26.9 us
  Pallas kernels  26.1 us (97%)
  local copies, waits for them, and re-layouts  0.8 us (3%)
    pallas_call x1, Pallas kernels, shards(): pl.pallas_call(functools.partial(kernel, nx, ny, nj, modes, width), out_s...  26.1 us
    unnamed x1, local copies, waits for them, and re-layouts  0.8 us

profile of v4, /device:TPU:1, one launch (start us, length us, event | category | flops | bytes accessed | tf_op | source)
XLA Modules:
  0.0 26.9 jit_solution(10109436177729331239)
XLA Ops:
  0.0 26.1 %shard_map.82 = bf16[128,2048]{1,0:T(8,128)(2,1)S(1)} custom-call(bf16[128,2048]{1,0:T(8,128)(2,1)} %x_hbm.1, f32[16,2048]{1,0:T(8,128)} %bitcast.4, f32[16,2048]{1,0:T(8,128)} %bitcast.5, f32[16,128]{1,0:T(8,128)} %bitcast.6, f32[16,128]{1,0:T(8,128)} %bitcast.7, bf16[128,2048]{1,0:T(8,128)(2,1)} %gate_hbm.1, bf16[256,256]{1,0:T(8,128)(2,1)} %constant.4.clone.fwd_hbm, ...), custom_call_target="tpu_custom_call" | custom-call | tf_op jit(solution)/shard_map/pallas_call | solution.py:392
  26.1 0.8 %copy.10 = bf16[128,2048]{1,0:T(8,128)(2,1)} copy(bf16[128,2048]{1,0:T(8,128)(2,1)S(1)} %shard_map.82) | data formatting | bytes 1048576

commit v5 on v4

--- a/solution.py
+++ b/solution.py
@@ -168,9 +168,7 @@
             if t < tokens // 16 - 1:
                 terms = [a * c for a, c in zip(terms, jump)]
             both = jnp.concatenate([first, second], axis=0)
-            high = both.astype(BF16)
-            taps_v[t * 16:(t + 1) * 16, lanes] = high
-            taps_v[tokens + t * 16:tokens + (t + 1) * 16, lanes] = (both - high.astype(F32)).astype(BF16)
+            taps_v[t * 16:(t + 1) * 16, lanes] = both.astype(BF16)
         return carry
 
     lax.fori_loop(0, blocks, filter_block, 0)
@@ -235,24 +233,20 @@
         scale = jnp.concatenate([scol_v[...]] * per, axis=1)
         gain = jnp.concatenate([gain_v[pl.ds(c * per + n, 1), :] for n in range(per)], axis=1)
         xn = (x_v[:, lanes].astype(F32) * scale * gain).astype(BF16)
-        high = taps_v[:tokens, lanes]
-        low = taps_v[tokens:, lanes]
+        taps = taps_v[:, lanes]
         spec = jnp.dot(fwd_v[...], jnp.concatenate([xn, xn], axis=0), preferred_element_type=F32)
-        filt = jnp.dot(fwd_v[...], jnp.concatenate([high, high], axis=0), preferred_element_type=F32)
-        filt = filt + jnp.dot(fwd_v[:, :tokens], low, preferred_element_type=F32)
+        filt = jnp.dot(fwd_v[...], jnp.concatenate([taps, taps], axis=0), preferred_element_type=F32)
         xr, xi = spec[:tokens], spec[tokens:]
         fr, fi = filt[:tokens], filt[tokens:]
         prod = jnp.concatenate([xr * fr - xi * fi, xr * fi + xi * fr], axis=0)
-        phigh = prod.astype(BF16)
-        plow = (prod - phigh.astype(F32)).astype(BF16)
-        conv = jnp.dot(inv_v[...], jnp.concatenate([phigh, phigh], axis=0), preferred_element_type=F32)
-        conv = conv + jnp.dot(inv_v[:, :2 * tokens], plow, preferred_element_type=F32)
+        prod = prod.astype(BF16)
+        conv = jnp.dot(inv_v[...], jnp.concatenate([prod, prod], axis=0), preferred_element_type=F32)
         skip = jnp.concatenate([skip_v[pl.ds(c * per + n, 1), :] for n in range(per)], axis=1)
         conv_v[:, lanes] = conv + skip * xn.astype(F32)
         return carry
 
     chunks = chans // width
-    cut1, cut2 = chunks // 2, (3 * chunks) // 4
+    cut1, cut2 = (3 * chunks) // 8, (5 * chunks) // 8
     lax.fori_loop(0, cut1, local_conv, 0)
 
     own = pl.ds(pl.multiple_of(mj * LANES, LANES), LANES)
@@ -342,8 +336,7 @@
 
     lax.fori_loop(0, nj, drain_states, 0)
 
-    def finish_block(i, carry):
-        b = lax.rem(mj + 2 * nj - spread(nj - 1 - i), nj)
+    def await_block(b):
 
         @pl.when(b != mj)
         def _():
@@ -351,6 +344,7 @@
                 src_ref=ca_out.at[b], dst_ref=ca_in.at[b], send_sem=ca_send.at[b], recv_sem=ca_recv.at[b],
                 device_id=group_peer(b), device_id_type=MESH).wait_recv()
 
+    def finish(b):
         lanes = pl.ds(pl.multiple_of(b * LANES, LANES), LANES)
         jump = rows_of(jump_v[:, lanes])
         weight = ca_in[b].astype(F32)
@@ -364,6 +358,13 @@
             both = jnp.concatenate([first, second], axis=0) + conv_v[t * 16:(t + 1) * 16, lanes]
             gate = gate_v[t * 16:(t + 1) * 16, lanes].astype(F32)
             out_ref[t * 16:(t + 1) * 16, lanes] = (both * gate).astype(BF16)
+
+    def finish_blocks(i, carry):
+        pair = [lax.rem(mj + 2 * nj - spread(nj - 1 - 2 * i - n), nj) for n in range(2)]
+        for b in pair:
+            await_block(b)
+        for b in pair:
+            finish(b)
         return carry
 
     def drain_carries(k, carry):
@@ -373,9 +374,9 @@
 
         return carry
 
-    lax.fori_loop(0, blocks // 4, finish_block, 0)
+    lax.fori_loop(0, blocks // 8, finish_blocks, 0)
     lax.fori_loop(0, nj, drain_carries, 0)
-    lax.fori_loop(blocks // 4, blocks, finish_block, 0)
+    lax.fori_loop(blocks // 8, blocks // 2, finish_blocks, 0)
 
 
 def shards(nx, nseq, stream, norm_gain, gate_act, decay_rate, residue, skip_gain):
@@ -407,7 +408,7 @@
             vmem((nx, 8, LANES), F32),
             vmem((tokens, LANES), F32),
             vmem((blocks * modes, 8, LANES), F32),
-            vmem((2 * tokens, chans), BF16),
+            vmem((tokens, chans), BF16),
             vmem((tokens, chans), F32),
             vmem((blocks * modes, 8, LANES), F32),
             vmem((modes, chans), F32),

time: 27 us -> 26.8 us (level)
  no operation moved by 1% of the time
where the time goes in v5:
time: 26.8 us; the launch traced here: 26.7 us
  Pallas kernels  25.9 us (97%)
  local copies, waits for them, and re-layouts  0.8 us (3%)
    pallas_call x1, Pallas kernels, shards(): pl.pallas_call(functools.partial(kernel, nx, ny, nj, modes, width), out_s...  25.9 us
    unnamed x1, local copies, waits for them, and re-layouts  0.8 us

profile of v5, /device:TPU:1, one launch (start us, length us, event | category | flops | bytes accessed | tf_op | source)
XLA Modules:
  0.0 26.7 jit_solution(17671762078722127794)
XLA Ops:
  0.0 25.9 %shard_map.82 = bf16[128,2048]{1,0:T(8,128)(2,1)S(1)} custom-call(bf16[128,2048]{1,0:T(8,128)(2,1)} %x_hbm.1, f32[16,2048]{1,0:T(8,128)} %bitcast.4, f32[16,2048]{1,0:T(8,128)} %bitcast.5, f32[16,128]{1,0:T(8,128)} %bitcast.6, f32[16,128]{1,0:T(8,128)} %bitcast.7, bf16[128,2048]{1,0:T(8,128)(2,1)} %gate_hbm.1, bf16[256,256]{1,0:T(8,128)(2,1)} %constant.4.clone.fwd_hbm, ...), custom_call_target="tpu_custom_call" | custom-call | tf_op jit(solution)/shard_map/pallas_call | solution.py:393
  25.9 0.8 %copy.10 = bf16[128,2048]{1,0:T(8,128)(2,1)} copy(bf16[128,2048]{1,0:T(8,128)(2,1)S(1)} %shard_map.82) | data formatting | bytes 1048576

commit v6 on v5

--- a/solution.py
+++ b/solution.py
@@ -222,10 +222,15 @@
         pl.semaphore_wait(barrier, nj // 2)
 
         def send_state(i, carry):
-            state_copy(lax.rem(mj + spread(i), nj)).start()
+            k = nj - 1 - i
+
+            @pl.when(k != mj)
+            def _():
+                state_copy(k).start()
+
             return carry
 
-        lax.fori_loop(0, nj - 1, send_state, 0)
+        lax.fori_loop(0, nj, send_state, 0)
 
     def local_conv(c, carry):
         lanes = pl.ds(pl.multiple_of(c * width, width), width)
@@ -246,7 +251,7 @@
         return carry
 
     chunks = chans // width
-    cut1, cut2 = (3 * chunks) // 8, (5 * chunks) // 8
+    cut1, cut2 = (3 * chunks) // 8, (4 * chunks) // 8
     lax.fori_loop(0, cut1, local_conv, 0)
 
     own = pl.ds(pl.multiple_of(mj * LANES, LANES), LANES)
@@ -305,11 +310,10 @@
             src_ref=ca_out.at[k], dst_ref=ca_in.at[mj], send_sem=ca_send.at[k], recv_sem=ca_recv.at[mj],
             device_id=group_peer(k), device_id_type=MESH)
 
-    def send_carry(i, carry):
-        k = lax.rem(mj + spread(i), nj)
+    def send_carry(k, carry):
         ca_out[k] = (pre_v[k] + fac_v[k] * before).astype(ca_out.dtype)
 
-        @pl.when(i < nj - 1)
+        @pl.when(k != mj)
         def _():
             carry_copy(k).start()
 

time: 26.8 us -> 26.6 us (level); the launches traced: 26.7 us -> 26.1 us
  Pallas kernels: 25.9 us -> 25.3 us
    pallas_call x1, Pallas kernels: 25.9 us -> 25.3 us  [shards(): pl.pallas_call(functools.partial(kernel, nx, ny, nj, modes, width), out_s...]
where the time goes in v6:
time: 26.6 us; the launch traced here: 26.1 us
  Pallas kernels  25.3 us (95%)
  local copies, waits for them, and re-layouts  0.8 us (3%)
    pallas_call x1, Pallas kernels, shards(): pl.pallas_call(functools.partial(kernel, nx, ny, nj, modes, width), out_s...  25.3 us
    unnamed x1, local copies, waits for them, and re-layouts  0.8 us

profile of v6, /device:TPU:1, one launch (start us, length us, event | category | flops | bytes accessed | tf_op | source)
XLA Modules:
  0.0 26.1 jit_solution(625144911852185333)
XLA Ops:
  0.0 25.3 %shard_map.82 = bf16[128,2048]{1,0:T(8,128)(2,1)S(1)} custom-call(bf16[128,2048]{1,0:T(8,128)(2,1)} %x_hbm.1, f32[16,2048]{1,0:T(8,128)} %bitcast.4, f32[16,2048]{1,0:T(8,128)} %bitcast.5, f32[16,128]{1,0:T(8,128)} %bitcast.6, f32[16,128]{1,0:T(8,128)} %bitcast.7, bf16[128,2048]{1,0:T(8,128)(2,1)} %gate_hbm.1, bf16[256,256]{1,0:T(8,128)(2,1)} %constant.4.clone.fwd_hbm, ...), custom_call_target="tpu_custom_call" | custom-call | tf_op jit(solution)/shard_map/pallas_call | solution.py:397
  25.3 0.8 %copy.10 = bf16[128,2048]{1,0:T(8,128)(2,1)} copy(bf16[128,2048]{1,0:T(8,128)(2,1)S(1)} %shard_map.82) | data formatting | bytes 1048576

commit v7 on v6

--- a/solution.py
+++ b/solution.py
@@ -108,6 +108,11 @@
     def _():
         greet(half)
 
+    @pl.when(jnp.logical_not(late))
+    def _():
+        pl.semaphore_wait(barrier, nx + ny - 2)
+        greet(half)
+
     tiles_part = rows_part // 16
     for p in range(parts):
         rows = pl.ds(p * rows_part, rows_part)
@@ -130,11 +135,6 @@
     def _():
         pl.semaphore_wait(barrier, nx + ny + nj - 3)
         greet(0)
-
-    @pl.when(jnp.logical_not(late))
-    def _():
-        pl.semaphore_wait(barrier, nx + ny - 2)
-        greet(half)
 
     sq_copies = []
     for d in range(1, nx):
@@ -251,7 +251,7 @@
         return carry
 
     chunks = chans // width
-    cut1, cut2 = (3 * chunks) // 8, (4 * chunks) // 8
+    cut1, cut2 = (3 * chunks) // 8, (3 * chunks) // 8
     lax.fori_loop(0, cut1, local_conv, 0)
 
     own = pl.ds(pl.multiple_of(mj * LANES, LANES), LANES)

time: 26.6 us -> 26.6 us (level)
  the two profiles are of different devices: /device:TPU:1 before, /device:TPU:9 now
where the time goes in v7:
time: 26.6 us; the launch traced here: 26.5 us
  Pallas kernels  25.7 us (97%)
  local copies, waits for them, and re-layouts  0.8 us (3%)
    pallas_call x1, Pallas kernels, shards(): pl.pallas_call(functools.partial(kernel, nx, ny, nj, modes, width), out_s...  25.7 us
    unnamed x1, local copies, waits for them, and re-layouts  0.8 us

profile of v7, /device:TPU:9, one launch (start us, length us, event | category | flops | bytes accessed | tf_op | source)
XLA Modules:
  0.0 26.5 jit_solution(9656383433837722263)
XLA Ops:
  0.0 25.7 %shard_map.82 = bf16[128,2048]{1,0:T(8,128)(2,1)S(1)} custom-call(bf16[128,2048]{1,0:T(8,128)(2,1)} %x_hbm.1, f32[16,2048]{1,0:T(8,128)} %bitcast.4, f32[16,2048]{1,0:T(8,128)} %bitcast.5, f32[16,128]{1,0:T(8,128)} %bitcast.6, f32[16,128]{1,0:T(8,128)} %bitcast.7, bf16[128,2048]{1,0:T(8,128)(2,1)} %gate_hbm.1, bf16[256,256]{1,0:T(8,128)(2,1)} %constant.4.clone.fwd_hbm, ...), custom_call_target="tpu_custom_call" | custom-call | tf_op jit(solution)/shard_map/pallas_call | solution.py:397
  25.7 0.8 %copy.10 = bf16[128,2048]{1,0:T(8,128)(2,1)} copy(bf16[128,2048]{1,0:T(8,128)(2,1)S(1)} %shard_map.82) | data formatting | bytes 1048576

commit v8 on v7

--- a/solution.py
+++ b/solution.py
@@ -378,9 +378,9 @@
 
         return carry
 
-    lax.fori_loop(0, blocks // 8, finish_blocks, 0)
+    lax.fori_loop(0, blocks // 4, finish_blocks, 0)
     lax.fori_loop(0, nj, drain_carries, 0)
-    lax.fori_loop(blocks // 8, blocks // 2, finish_blocks, 0)
+    lax.fori_loop(blocks // 4, blocks // 2, finish_blocks, 0)
 
 
 def shards(nx, nseq, stream, norm_gain, gate_act, decay_rate, residue, skip_gain):

time: 26.6 us -> 26.6 us (level)
  no operation moved by 1% of the time
where the time goes in v8:
time: 26.6 us; the launch traced here: 26.5 us
  Pallas kernels  25.7 us (97%)
  local copies, waits for them, and re-layouts  0.8 us (3%)
    pallas_call x1, Pallas kernels, shards(): pl.pallas_call(functools.partial(kernel, nx, ny, nj, modes, width), out_s...  25.7 us
    unnamed x1, local copies, waits for them, and re-layouts  0.8 us

profile of v8, /device:TPU:9, one launch (start us, length us, event | category | flops | bytes accessed | tf_op | source)
XLA Modules:
  0.0 26.5 jit_solution(10962122915573279061)
XLA Ops:
  0.0 25.7 %shard_map.82 = bf16[128,2048]{1,0:T(8,128)(2,1)S(1)} custom-call(bf16[128,2048]{1,0:T(8,128)(2,1)} %x_hbm.1, f32[16,2048]{1,0:T(8,128)} %bitcast.4, f32[16,2048]{1,0:T(8,128)} %bitcast.5, f32[16,128]{1,0:T(8,128)} %bitcast.6, f32[16,128]{1,0:T(8,128)} %bitcast.7, bf16[128,2048]{1,0:T(8,128)(2,1)} %gate_hbm.1, bf16[256,256]{1,0:T(8,128)(2,1)} %constant.4.clone.fwd_hbm, ...), custom_call_target="tpu_custom_call" | custom-call | tf_op jit(solution)/shard_map/pallas_call | solution.py:397
  25.7 0.8 %copy.10 = bf16[128,2048]{1,0:T(8,128)(2,1)} copy(bf16[128,2048]{1,0:T(8,128)(2,1)S(1)} %shard_map.82) | data formatting | bytes 1048576
